TPU v7x, 256 devices: a whole 4x4x8 slice. The times are simulated.
256 devices in a mesh: dp: 16 (over y, x), expert: 16 (over z, core).
Axes of the slice: x: 4, y: 4, z: 8, core: 2. Of those that a mesh axis runs over, the one named last changes fastest.
Arguments:
- tokens: bfloat16 [8192, 2048], P('dp'), may hold values from -6 to 6
- routes: int32 [8192, 6], P('dp'), may hold values from 0 to 63, all different within a row; in each aligned block of 512 rows (0 to 511, 512 to 1023, ...) at most 72 rows name the same one
- route_weight: float32 [8192, 6], P('dp'), may hold values from 0.05 to 0.5
- w_gate: bfloat16 [256, 352, 2048], P(('dp', 'expert')), may hold values from -0.125 to 0.125
- w_up: bfloat16 [256, 352, 2048], P(('dp', 'expert')), may hold values from -0.125 to 0.125
- w_down: bfloat16 [256, 352, 2048], P(('dp', 'expert')), may hold values from -0.15625 to 0.15625
- grad_out: bfloat16 [8192, 2048], P(('dp', 'expert')), may hold values from -6 to 6
Outputs:
- mixed: bfloat16 [8192, 2048], P(('dp', 'expert'))
- grad_tokens: bfloat16 [8192, 2048], P(('dp', 'expert'))
- grad_route_weight: float32 [8192, 6], P(('dp', 'expert'))
- grad_gate: bfloat16 [256, 352, 2048], P(('dp', 'expert'))
- grad_up: bfloat16 [256, 352, 2048], P(('dp', 'expert'))
- grad_down: bfloat16 [256, 352, 2048], P(('dp', 'expert'))
Inputs may be any that keep to these rules, and one draw needn't show every extreme that they name: `routes`: each row names 6 different experts. Within the 512 rows of one index of dp no expert is named by more than 72 rows.
All inputs are finite; a program needn't handle non-finite values.
Results may differ from a plain program's by a relative error of at most 0.023.
Values may be sent and summed in bfloat16 or wider, within the bound.
A program may use at most 192 MiB of HBM per device.

v0:
```python
import jax
import jax.numpy as jnp
from jax import lax
from jax.sharding import PartitionSpec as P

SHARDS = 4


def silu_parts(gate_pre):
    sigma = jax.nn.sigmoid(gate_pre)
    return (gate_pre * sigma, sigma * (1.0 + gate_pre * (1.0 - sigma)))


def deliver(buffer):
    dp_count, slot_count, width = buffer.shape
    arrived = lax.all_to_all(buffer, "dp", split_axis=0, concat_axis=0, tiled=True)
    return arrived.reshape(dp_count * slot_count, width)


def send_back(rows, dp_count, slot_count):
    width = rows.shape[1]
    returned = lax.all_to_all(
        rows.reshape(dp_count, slot_count, width), "dp", split_axis=0, concat_axis=0, tiled=True
    )
    return (returned.reshape(dp_count * slot_count, width), jnp.zeros((), jnp.int32))


def body(tokens, routes, route_weight, w_gate, w_up, w_down, grad_out):
    dp_count = lax.axis_size("dp")
    ex_count = lax.axis_size("expert")
    groups = ex_count // SHARDS
    my_group = lax.axis_index("expert") // SHARDS
    tok_rows, top_count = routes.shape
    width = tokens.shape[1]
    expert_count = dp_count * groups
    capacity = min(tok_rows, 3 * tok_rows * top_count // (2 * expert_count))
    flat_routes = routes.reshape(-1)
    route_count = flat_routes.shape[0]
    owner_ids = jnp.arange(dp_count, dtype=jnp.int32) * groups + my_group
    hit_table = (flat_routes[:, None] == owner_ids[None, :]).astype(jnp.int32)
    is_live = jnp.sum(hit_table, axis=1)
    owner_dp = jnp.sum(hit_table * jnp.arange(dp_count, dtype=jnp.int32)[None, :], axis=1)
    slot_index = jnp.sum((jnp.cumsum(hit_table, axis=0) - 1) * hit_table, axis=1)
    dump_row = dp_count * capacity
    target = jnp.where(is_live == 1, owner_dp * capacity + slot_index, dump_row)
    source = (
        jnp.full((dump_row + 1,), route_count, jnp.int32)
        .at[target]
        .set(jnp.arange(route_count, dtype=jnp.int32))[:dump_row]
    )
    filled = source < route_count
    safe_source = jnp.where(filled, source, 0)
    token_of = safe_source // top_count
    weights_flat = route_weight.reshape(-1)
    send_rows = jnp.where(filled[:, None], tokens[token_of], jnp.zeros((), tokens.dtype))
    x_rows = deliver(send_rows.reshape(dp_count, capacity, width))
    gate_matrix = w_gate[0]
    up_matrix = w_up[0]
    down_matrix = w_down[0]
    gate_pre = jnp.einsum("rd,fd->rf", x_rows, gate_matrix, preferred_element_type=jnp.float32)
    up_pre = jnp.einsum("rd,fd->rf", x_rows, up_matrix, preferred_element_type=jnp.float32)
    silu_value, silu_slope = silu_parts(gate_pre)
    hidden = (silu_value * up_pre).astype(jnp.bfloat16)
    shard_part = jnp.dot(hidden, down_matrix, preferred_element_type=jnp.float32).astype(
        jnp.bfloat16
    )
    returned, offset = send_back(shard_part, dp_count, capacity)
    piece_width = returned.shape[1]
    safe_target = jnp.where(is_live == 1, target, 0)
    route_part = jnp.where(
        is_live[:, None] == 1, returned[safe_target], jnp.zeros((), returned.dtype)
    )
    weighted = weights_flat[:, None] * route_part.astype(jnp.float32)
    mixed_part = jnp.sum(weighted.reshape(tok_rows, top_count, piece_width), axis=1)
    cotangent = lax.all_gather(grad_out, "expert", axis=0, tiled=True)
    route_grad = jnp.sum(
        route_part.reshape(tok_rows, top_count, piece_width).astype(jnp.float32)
        * cotangent[:, None, :].astype(jnp.float32),
        axis=2,
    )
    weight_of = jnp.where(filled, weights_flat[safe_source], jnp.zeros((), weights_flat.dtype))
    send_cot = (weight_of[:, None] * cotangent[token_of].astype(jnp.float32)).astype(jnp.bfloat16)
    cot_rows = deliver(send_cot.reshape(dp_count, capacity, width))
    d_hidden = jnp.einsum("rd,fd->rf", cot_rows, down_matrix, preferred_element_type=jnp.float32)
    d_gate = (d_hidden * up_pre * silu_slope).astype(jnp.bfloat16)
    d_up = (d_hidden * silu_value).astype(jnp.bfloat16)
    grad_down = jnp.einsum(
        "rf,rd->fd", hidden, cot_rows, preferred_element_type=jnp.float32
    ).astype(jnp.bfloat16)[None]
    grad_gate = jnp.einsum("rf,rd->fd", d_gate, x_rows, preferred_element_type=jnp.float32).astype(
        jnp.bfloat16
    )[None]
    grad_up = jnp.einsum("rf,rd->fd", d_up, x_rows, preferred_element_type=jnp.float32).astype(
        jnp.bfloat16
    )[None]
    shard_dx = jnp.dot(d_gate, gate_matrix, preferred_element_type=jnp.float32) + jnp.dot(
        d_up, up_matrix, preferred_element_type=jnp.float32
    )
    dx_back, dx_offset = send_back(shard_dx.astype(jnp.bfloat16), dp_count, capacity)
    route_dx = jnp.where(is_live[:, None] == 1, dx_back[safe_target], jnp.zeros((), dx_back.dtype))
    dx_part = jnp.sum(
        route_dx.astype(jnp.float32).reshape(tok_rows, top_count, piece_width), axis=1
    )
    mixed, grad_tokens, grad_route = (
        lax.psum_scatter(
            mixed_part.astype(jnp.bfloat16), "expert", scatter_dimension=0, tiled=True
        ).astype(jnp.float32),
        lax.psum_scatter(
            dx_part.astype(jnp.bfloat16), "expert", scatter_dimension=0, tiled=True
        ).astype(jnp.float32),
        lax.psum_scatter(
            route_grad.astype(jnp.bfloat16), "expert", scatter_dimension=0, tiled=True
        ).astype(jnp.float32),
    )
    return (
        mixed.astype(jnp.bfloat16),
        grad_tokens.astype(jnp.bfloat16),
        grad_route,
        grad_gate,
        grad_up,
        grad_down,
    )


def solution(mesh):
    return jax.shard_map(
        body,
        mesh=mesh,
        in_specs=(
            P("dp", None),
            P("dp", None),
            P("dp", None),
            P(("dp", "expert"), None, None),
            P(("dp", "expert"), None, None),
            P(("dp", "expert"), None, None),
            P(("dp", "expert"), None),
        ),
        out_specs=(
            P(("dp", "expert"), None),
            P(("dp", "expert"), None),
            P(("dp", "expert"), None),
            P(("dp", "expert"), None, None),
            P(("dp", "expert"), None, None),
            P(("dp", "expert"), None, None),
        ),
        check_vma=False,
    )
```

profile of v0, /device:TPU:10, one launch (start us, length us, event | category | flops | bytes accessed | tf_op | source)
XLA Modules:
  0.0 591.3 jit_solution(7139322173893790338)
XLA Ops:
  14.9 11.8 %scatter_custom_fusion = s32[1153]{0:T(1024)S(1)} fusion(s32[3072]{0:T(1024)S(1)} %bitcast.66, s32[3072]{0:T(1024)S(1)} %iota.13, s32[]{:T(128)} %constant.52.clone.1), kind=kCustom, calls=%fused_computation.64 | custom fusion | bytes 4616 | tf_op jit(solution)/shard_map/scatter | solution.py:49
  26.8 6.0 %gather_fusion = bf16[1152,2048]{1,0:T(8,128)(2,1)} fusion(bf16[512,2048]{1,0:T(8,128)(2,1)S(1)} %copy-done, s32[2048]{0:T(1024)S(1)} %pad_clamp_fusion.1), kind=kCustom, calls=%fused_computation | custom fusion | bytes 9441792 | tf_op jit(solution)/shard_map/gather | solution.py:55
  37.7 7.5 %all-to-all-start = ((bf16[16,72,2048]{2,1,0:T(8,128)(2,1)}), bf16[16,72,2048]{2,1,0:T(8,128)(2,1)}, u32[]{:S(2)}, u32[]{:S(2)}) async-start(bf16[16,72,2048]{2,1,0:T(8,128)(2,1)} %broadcast_select_fusion), calls=%async_computation | async-start | bytes 9437184 | tf_op jit(solution)/shard_map/all_to_all | solution.py:16
  45.5 6.5 %gather_fusion.2 = f32[1152]{0:T(1024)S(1)} fusion(f32[3072]{0:T(1024)S(1)} %reshape.199, s32[2048]{0:T(1024)S(1)} %pad_clamp_fusion), kind=kCustom, calls=%fused_computation.2 | custom fusion | bytes 13824 | tf_op jit(solution)/shard_map/gather | solution.py:81
  52.5 12.5 %gather_fusion.3 = bf16[1152,2048]{1,0:T(8,128)(2,1)} fusion(bf16[512,2048]{1,0:T(8,128)(2,1)} %all-gather.2.cloned.1.call-done, s32[2048]{0:T(1024)S(1)} %pad_clamp_fusion.1), kind=kCustom, calls=%fused_computation.3 | custom fusion | bytes 9441792 | tf_op jit(solution)/shard_map/gather | solution.py:82
  70.3 40.9 %all-to-all-done = bf16[16,72,2048]{2,1,0:T(8,128)(2,1)} async-done(((bf16[16,72,2048]{2,1,0:T(8,128)(2,1)}), bf16[16,72,2048]{2,1,0:T(8,128)(2,1)}, u32[]{:S(2)}, u32[]{:S(2)}) %all-to-all-start) | async-done | bytes 4718624 | tf_op jit(solution)/shard_map/all_to_all | solution.py:16
  111.2 9.9 %all-to-all-start.2 = ((bf16[16,72,2048]{2,1,0:T(8,128)(2,1)}), bf16[16,72,2048]{2,1,0:T(8,128)(2,1)}, u32[]{:S(2)}, u32[]{:S(2)}) async-start(bf16[16,72,2048]{2,1,0:T(8,128)(2,1)} %fusion), calls=%async_computation.3 | async-start | bytes 9437184 | tf_op jit(solution)/shard_map/all_to_all | solution.py:16
  121.2 5.7 fusion.10
  132.4 50.6 %all-to-all-done.2 = bf16[16,72,2048]{2,1,0:T(8,128)(2,1)} async-done(((bf16[16,72,2048]{2,1,0:T(8,128)(2,1)}), bf16[16,72,2048]{2,1,0:T(8,128)(2,1)}, u32[]{:S(2)}, u32[]{:S(2)}) %all-to-all-start.2) | async-done | bytes 4718624 | tf_op jit(solution)/shard_map/all_to_all | solution.py:16
  183.0 7.1 %multiply_convert_fusion = (bf16[1152,352]{0,1:T(8,128)(2,1)}, bf16[1152,352]{0,1:T(8,128)(2,1)S(1)}, bf16[1152,352]{0,1:T(8,128)(2,1)S(1)}) fusion(f32[1152,352]{0,1:T(8,128)} %fusion.14, f32[1152,352]{0,1:T(8,128)} %fusion.10, bf16[1152,2048]{1,0:T(8,128)(2,1)} %bitcast.12, bf16[1,352,2048]{2,1,0:T(8,128)(2,1)} %param.12), kind=kOutput, calls=%fused_computation.21 | convolution fusion | flops 1667026944 | bytes 11837440 | tf_op jit(solution)/shard_map/rd,fd->rf/dot_general | solution.py:84
  194.4 10.9 %all-to-all-start.1 = ((bf16[16,72,2048]{2,1,0:T(8,128)(2,1)}), bf16[16,72,2048]{2,1,0:T(8,128)(2,1)}, u32[]{:S(2)}, u32[]{:S(2)}) async-start(bf16[16,72,2048]{2,1,0:T(8,128)(2,1)} %bitcast.61), calls=%async_computation.1 | async-start | bytes 9437184 | tf_op jit(solution)/shard_map/all_to_all | solution.py:22
  212.4 50.8 %all-to-all-done.1 = bf16[16,72,2048]{2,1,0:T(8,128)(2,1)} async-done(((bf16[16,72,2048]{2,1,0:T(8,128)(2,1)}), bf16[16,72,2048]{2,1,0:T(8,128)(2,1)}, u32[]{:S(2)}, u32[]{:S(2)}) %all-to-all-start.1) | async-done | bytes 4718624 | tf_op jit(solution)/shard_map/all_to_all | solution.py:22
  263.2 11.3 %all-to-all-start.3 = ((bf16[16,72,2048]{2,1,0:T(8,128)(2,1)}), bf16[16,72,2048]{2,1,0:T(8,128)(2,1)}, u32[]{:S(2)}, u32[]{:S(2)}) async-start(bf16[16,72,2048]{2,1,0:T(8,128)(2,1)} %bitcast.59), calls=%async_computation.4 | async-start | bytes 9437184 | tf_op jit(solution)/shard_map/all_to_all | solution.py:22
  275.1 11.3 %mul.105 = f32[512,6,2048]{2,1,0:T(8,128)} broadcast(bf16[512,2048]{1,0:T(8,128)(2,1)S(1)} %copy-done.2), dimensions={0,2} | broadcast | bytes 27262976 | tf_op jit(solution)/shard_map/mul | solution.py:77
  286.4 29.5 %mul.106 = f32[3072,2048]{1,0:T(8,128)} reshape(f32[512,6,2048]{2,1,0:T(8,128)} %mul.105) | data formatting | bytes 50331648 | tf_op jit(solution)/shard_map/mul | solution.py:77
  315.9 26.8 %gather_fusion.1 = bf16[3072,2048]{1,0:T(8,128)(2,1)} fusion(bf16[1152,2048]{1,0:T(8,128)(2,1)} %bitcast.9, s32[3072]{0:T(1024)S(1)} %broadcast_clamp_fusion), kind=kCustom, calls=%fused_computation.1 | custom fusion | bytes 25178112 | tf_op jit(solution)/shard_map/gather | solution.py:71
  342.7 26.8 %gather_fusion.4 = bf16[3072,2048]{1,0:T(8,128)(2,1)} fusion(bf16[1152,2048]{1,0:T(8,128)(2,1)} %bitcast.14, s32[3072]{0:T(1024)S(1)} %broadcast_clamp_fusion), kind=kCustom, calls=%fused_computation.4 | custom fusion | bytes 25178112 | tf_op jit(solution)/shard_map/gather | solution.py:100
  369.5 20.4 %gather.31 = bf16[512,6,2048]{2,1,0:T(8,128)(2,1)} reshape(bf16[3072,2048]{1,0:T(8,128)(2,1)} %gather_fusion.4) | data formatting | bytes 25165824 | tf_op jit(solution)/shard_map/gather | solution.py:100
  389.8 13.1 %multiply_reduce_fusion.1 = bf16[3072]{0:T(1024)(128)(2,1)S(1)} fusion(f32[3072,2048]{1,0:T(8,128)} %mul.106, bf16[3072,2048]{1,0:T(8,128)(2,1)} %gather_fusion.1, pred[3072]{0:T(1024)(128)(4,1)S(1)} %broadcast_compare_fusion), kind=kLoop, calls=%fused_computation.7 | loop fusion | flops 25162752 | bytes 37757952 | tf_op jit(solution)/shard_map/reduce_sum | solution.py:76
  403.9 14.3 %select_reduce_fusion = bf16[512,2048]{1,0:T(8,128)(2,1)} fusion(bf16[512,6,2048]{2,1,0:T(8,128)(2,1)} %gather.31, pred[512,6]{1,0:T(8,128)(4,1)S(1)} %eq.59), kind=kLoop, calls=%fused_computation.8 | loop fusion | flops 11534336 | bytes 14683136 | tf_op jit(solution)/shard_map/reduce_sum | solution.py:101
  418.6 20.4 %gather.26 = bf16[512,6,2048]{2,1,0:T(8,128)(2,1)} reshape(bf16[3072,2048]{1,0:T(8,128)(2,1)} %gather_fusion.1) | data formatting | bytes 25165824 | tf_op jit(solution)/shard_map/gather | solution.py:71
  438.9 20.6 %multiply_reduce_fusion = bf16[512,2048]{1,0:T(8,128)(2,1)} fusion(bf16[512,6,2048]{2,1,0:T(8,128)(2,1)} %gather.26, f32[512,6]{1,0:T(8,128)S(1)} %copy-done.4, pred[512,6]{1,0:T(8,128)(4,1)S(1)} %eq.59), kind=kLoop, calls=%fused_computation.6 | loop fusion | flops 24117248 | bytes 14695424 | tf_op jit(solution)/shard_map/reduce_sum | solution.py:74
  477.6 46.1 %reduce-scatter.6.cloned.1.call-done = bf16[32,2048]{1,0:T(8,128)(2,1)} async-done(((bf16[512,2048]{1,0:T(8,128)(2,1)}), bf16[32,2048]{1,0:T(8,128)(2,1)}) %reduce-scatter.6.cloned.1.call-update) | async-done | bytes 131088 | tf_op jit(solution)/shard_map/reduce_scatter | solution.py:108
  523.7 61.0 %reduce-scatter.4.cloned.1.call-done = bf16[32,2048]{1,0:T(8,128)(2,1)} async-done(((bf16[512,2048]{1,0:T(8,128)(2,1)}), bf16[32,2048]{1,0:T(8,128)(2,1)}) %reduce-scatter.4.cloned.1.call-update) | async-done | bytes 131088 | tf_op jit(solution)/shard_map/reduce_scatter | solution.py:105
  (75 shorter events, 55.6 us)
Async XLA Ops:
  7.2 19.6 %copy-start = (bf16[512,2048]{1,0:T(8,128)(2,1)S(1)}, bf16[512,2048]{1,0:T(8,128)(2,1)}, u32[]{:S(2)}) copy-start(bf16[512,2048]{1,0:T(8,128)(2,1)} %param.7) | copy-start | bytes 6291460
  7.2 45.3 %all-gather.2.cloned.1.call-start = ((), (), s32[]{:S(2)}) async-start(), calls=%async_computation.8 | async-start | bytes 2228224 | tf_op jit(solution)/shard_map/all_gather | solution.py:75
  37.7 7.5 %copy-start.10 = (f32[512,6]{0,1:T(8,128)S(1)}, f32[512,6]{0,1:T(8,128)}, u32[]{:S(2)}) copy-start(f32[512,6]{0,1:T(8,128)} %param.9) | copy-start | bytes 36868
  37.7 73.5 %all-to-all-start = ((bf16[16,72,2048]{2,1,0:T(8,128)(2,1)}), bf16[16,72,2048]{2,1,0:T(8,128)(2,1)}, u32[]{:S(2)}, u32[]{:S(2)}) async-start(bf16[16,72,2048]{2,1,0:T(8,128)(2,1)} %broadcast_select_fusion), calls=%async_computation | async-start | bytes 9437184 | tf_op jit(solution)/shard_map/all_to_all | solution.py:16
  45.3 19.6 %copy-start.3 = (f32[512,6]{1,0:T(8,128)}, f32[512,6]{1,0:T(8,128)S(1)}, u32[]{:S(2)}) copy-start(f32[512,6]{1,0:T(8,128)S(1)} %copy.14) | copy-start | bytes 36868
  70.3 50.8 %copy-start.6 = (bf16[1,352,2048]{2,1,0:T(8,128)(2,1)S(1)}, bf16[1,352,2048]{2,1,0:T(8,128)(2,1)}, u32[]{:S(2)}) copy-start(bf16[1,352,2048]{2,1,0:T(8,128)(2,1)} %param.11) | copy-start | bytes 4325380
  111.2 71.8 %all-to-all-start.2 = ((bf16[16,72,2048]{2,1,0:T(8,128)(2,1)}), bf16[16,72,2048]{2,1,0:T(8,128)(2,1)}, u32[]{:S(2)}, u32[]{:S(2)}) async-start(bf16[16,72,2048]{2,1,0:T(8,128)(2,1)} %fusion), calls=%async_computation.3 | async-start | bytes 9437184 | tf_op jit(solution)/shard_map/all_to_all | solution.py:16
  121.1 5.7 copy-start.5
  183.0 7.1 %copy-start.11 = (bf16[1,352,2048]{2,1,0:T(8,128)(2,1)S(1)}, bf16[1,352,2048]{2,1,0:T(8,128)(2,1)}, u32[]{:S(2)}) copy-start(bf16[1,352,2048]{2,1,0:T(8,128)(2,1)} %param.12) | copy-start | bytes 4325380
  190.1 4.3 copy-start.12
  194.4 68.8 %all-to-all-start.1 = ((bf16[16,72,2048]{2,1,0:T(8,128)(2,1)}), bf16[16,72,2048]{2,1,0:T(8,128)(2,1)}, u32[]{:S(2)}, u32[]{:S(2)}) async-start(bf16[16,72,2048]{2,1,0:T(8,128)(2,1)} %bitcast.61), calls=%async_computation.1 | async-start | bytes 9437184 | tf_op jit(solution)/shard_map/all_to_all | solution.py:22
  205.3 2.7 copy-start.7
  205.3 2.7 copy-start.8
  263.2 11.9 %copy-start.2 = (bf16[512,2048]{1,0:T(8,128)(2,1)S(1)}, bf16[512,2048]{1,0:T(8,128)(2,1)}, u32[]{:S(2)}) copy-start(bf16[512,2048]{1,0:T(8,128)(2,1)} %all-gather.2.cloned.1.call-done) | copy-start | bytes 6291460
  263.2 79.5 %all-to-all-start.3 = ((bf16[16,72,2048]{2,1,0:T(8,128)(2,1)}), bf16[16,72,2048]{2,1,0:T(8,128)(2,1)}, u32[]{:S(2)}, u32[]{:S(2)}) async-start(bf16[16,72,2048]{2,1,0:T(8,128)(2,1)} %bitcast.59), calls=%async_computation.4 | async-start | bytes 9437184 | tf_op jit(solution)/shard_map/all_to_all | solution.py:22
  274.5 201.7 %reduce-scatter.8.cloned.1.call-start = ((), (), s32[]{:S(2)}) async-start(), calls=%async_computation.10 | async-start | bytes 139264 | tf_op jit(solution)/shard_map/reduce_scatter | solution.py:111
  403.9 119.8 %reduce-scatter.6.cloned.1.call-start = ((), (), s32[]{:S(2)}) async-start(), calls=%async_computation.9 | async-start | bytes 2228224 | tf_op jit(solution)/shard_map/reduce_scatter | solution.py:108
  418.2 20.7 %copy-start.4 = (f32[512,6]{1,0:T(8,128)S(1)}, f32[512,6]{1,0:T(8,128)}, u32[]{:S(2)}) copy-start(f32[512,6]{1,0:T(8,128)} %copy-done.3) | copy-start | bytes 36868
  418.3 166.5 %reduce-scatter.4.cloned.1.call-start = ((), (), s32[]{:S(2)}) async-start(), calls=%async_computation.7 | async-start | bytes 2228224 | tf_op jit(solution)/shard_map/reduce_scatter | solution.py:105
  438.9 20.6 %copy-start.13 = (bf16[1152,352]{0,1:T(8,128)(2,1)S(1)}, bf16[1152,352]{0,1:T(8,128)(2,1)}, u32[]{:S(2)}) copy-start(bf16[1152,352]{0,1:T(8,128)(2,1)} %copy-done.12) | copy-start | bytes 2433028
  459.6 5.6 copy-start.9
  465.1 119.6 %copy-start.1 = (bf16[512,2048]{1,0:T(8,128)(2,1)S(1)}, bf16[512,2048]{1,0:T(8,128)(2,1)}, u32[]{:S(2)}) copy-start(bf16[512,2048]{1,0:T(8,128)(2,1)} %param.7) | copy-start | bytes 6291460
Sparse Core Ops, SparseCore 0:
  9.8 42.5 all-gather.1
  404.0 58.6 reduce-scatter.7
  465.9 57.7 reduce-scatter.5
  526.8 57.8 reduce-scatter.3
where the time goes:
time: 594 us; the launch traced here: 591 us
  waiting for transfers between devices  250 us (42%)
  local copies, waits for them, and re-layouts  177 us (30%)
  other arithmetic  63.5 us (11%)
  matrix products  46.4 us (8%)
  starting transfers between devices  40.3 us (7%)
  between operations  14.1 us (2%)
    all_to_all x2, waiting for transfers between devices, deliver(): lax.all_to_all(buffer, 'dp', split_axis=0, concat_axis=0, tiled=True)  91.5 us
    reduce_scatter x1, waiting for transfers between devices, body(): lax.psum_scatter(mixed_part.astype(jnp.bfloat16), 'expert', scatter_dimen...  61 us
    all_to_all x2, waiting for transfers between devices, send_back(): lax.all_to_all(rows.reshape(dp_count, slot_count, width), 'dp', split_axi...  50.8 us
    gather x2, local copies, waits for them, and re-layouts, body(): returned[safe_target]  47.2 us
    gather x2, local copies, waits for them, and re-layouts, body(): dx_back[safe_target]  47.1 us
    reduce_scatter x1, waiting for transfers between devices, body(): lax.psum_scatter(dx_part.astype(jnp.bfloat16), 'expert', scatter_dimensio...  46.1 us
    mul x2, local copies, waits for them, and re-layouts, body(): route_part.reshape(tok_rows, top_count, piece_width).astype(jnp.float32)  40.8 us
    all_to_all x2, starting transfers between devices, send_back(): lax.all_to_all(rows.reshape(dp_count, slot_count, width), 'dp', split_axi...  22.2 us
  transfers between devices with their start and end apart: 8, of which 6 were waited for; matrix products, arithmetic and copies ran while one was open for 36% of the time, Pallas kernels for 0%

commit v1 on v0

--- a/solution.py
+++ b/solution.py
@@ -4,6 +4,29 @@
 from jax.sharding import PartitionSpec as P
 
 SHARDS = 4
+
+
+def in_blocks(x, dim, size):
+    shape = x.shape
+    blocks = x.reshape(*shape[:dim], size, shape[dim] // size, *shape[dim + 1 :])
+    return jnp.moveaxis(blocks, dim, 0)
+
+
+def in_order(blocks, dim):
+    blocks = jnp.moveaxis(blocks, 0, dim)
+    shape = blocks.shape
+    return blocks.reshape(*shape[:dim], shape[dim] * shape[dim + 1], *shape[dim + 2 :])
+
+
+def exchange_in_pairs(shard, axis, split_dim, concat_dim):
+    count, index = (lax.axis_size(axis), lax.axis_index(axis))
+    blocks = in_blocks(shard, split_dim, count)
+    done = [blocks[index]]
+    for lap in range(1, count):
+        sent = blocks[index ^ lap]
+        done.append(lax.ppermute(sent, axis, [(i, i ^ lap) for i in range(count)]))
+    blocks = jnp.stack(done)[index ^ jnp.arange(count)]
+    return in_order(blocks, concat_dim)
 
 
 def silu_parts(gate_pre):
@@ -19,9 +42,7 @@
 
 def send_back(rows, dp_count, slot_count):
     width = rows.shape[1]
-    returned = lax.all_to_all(
-        rows.reshape(dp_count, slot_count, width), "dp", split_axis=0, concat_axis=0, tiled=True
-    )
+    returned = exchange_in_pairs(rows.reshape(dp_count, slot_count, width), "dp", 0, 0)
     return (returned.reshape(dp_count * slot_count, width), jnp.zeros((), jnp.int32))
 
 

time: 594 us -> 747 us (1.26)
  starting transfers between devices: 40.3 us -> 101 us
  waiting for transfers between devices: 250 us -> 298 us
  local copies, waits for them, and re-layouts: 177 us -> 218 us
    ppermute x0 -> x30, waiting for transfers between devices: none -> 139 us  [exchange_in_pairs(): done.append(lax.ppermute(sent, axis, [(i, i ^ lap) for i in range(count)]))]
    ppermute x0 -> x30, starting transfers between devices: none -> 82.7 us  [exchange_in_pairs(): done.append(lax.ppermute(sent, axis, [(i, i ^ lap) for i in range(count)]))]
    all_to_all x2 -> x0, waiting for transfers between devices: 50.8 us -> none  [send_back(): lax.all_to_all(rows.reshape(dp_count, slot_count, width), 'dp', split_axi...]
    all_to_all x2, waiting for transfers between devices: 91.5 us -> 48.5 us  [deliver(): lax.all_to_all(buffer, 'dp', split_axis=0, concat_axis=0, tiled=True)]
    unnamed x31 -> x61, local copies, waits for them, and re-layouts: 2.44 us -> 26.9 us
    all_to_all x2 -> x0, starting transfers between devices: 22.2 us -> none  [send_back(): lax.all_to_all(rows.reshape(dp_count, slot_count, width), 'dp', split_axi...]
    gather x0 -> x2, local copies, waits for them, and re-layouts: none -> 11 us  [exchange_in_pairs(): blocks = jnp.stack(done)[index ^ jnp.arange(count)]]
  transfers between devices with their start and end apart: 8 -> 36, of which waited for: 6 -> 27; matrix products, arithmetic and copies ran while one was open for 36% -> 30% of each run, Pallas kernels for 0% -> 0%
where the time goes in v1:
time: 747 us; the launch traced here: 738 us
  waiting for transfers between devices  298 us (40%)
  local copies, waits for them, and re-layouts  218 us (29%)
  starting transfers between devices  101 us (14%)
  other arithmetic  64.1 us (9%)
  matrix products  42.7 us (6%)
  between operations  14.4 us (2%)
    ppermute x30, waiting for transfers between devices, exchange_in_pairs(): done.append(lax.ppermute(sent, axis, [(i, i ^ lap) for i in range(count)]))  139 us
    ppermute x30, starting transfers between devices, exchange_in_pairs(): done.append(lax.ppermute(sent, axis, [(i, i ^ lap) for i in range(count)]))  82.7 us
    reduce_scatter x1, waiting for transfers between devices, body(): lax.psum_scatter(mixed_part.astype(jnp.bfloat16), 'expert', scatter_dimen...  61 us
    all_to_all x2, waiting for transfers between devices, deliver(): lax.all_to_all(buffer, 'dp', split_axis=0, concat_axis=0, tiled=True)  48.5 us
    reduce_scatter x1, waiting for transfers between devices, body(): lax.psum_scatter(dx_part.astype(jnp.bfloat16), 'expert', scatter_dimensio...  48.3 us
    gather x2, local copies, waits for them, and re-layouts, body(): returned[safe_target]  47.2 us
    gather x2, local copies, waits for them, and re-layouts, body(): dx_back[safe_target]  47.1 us
    mul x2, local copies, waits for them, and re-layouts, body(): route_part.reshape(tok_rows, top_count, piece_width).astype(jnp.float32)  41 us
  transfers between devices with their start and end apart: 36, of which 27 were waited for; matrix products, arithmetic and copies ran while one was open for 30% of the time, Pallas kernels for 0%

profile of v1, /device:TPU:10, one launch (start us, length us, event | category | flops | bytes accessed | tf_op | source)
XLA Modules:
  0.0 738.0 jit_solution(164620846524609772)
XLA Ops:
  14.9 11.8 %scatter_custom_fusion = s32[1153]{0:T(1024)S(1)} fusion(s32[3072]{0:T(1024)S(1)} %bitcast.193, s32[3072]{0:T(1024)S(1)} %iota.18, s32[]{:T(128)} %constant.35.clone.1), kind=kCustom, calls=%fused_computation.129 | custom fusion | bytes 4616 | tf_op jit(solution)/shard_map/scatter | solution.py:70
  37.7 7.5 %all-to-all-start = ((bf16[16,72,2048]{2,1,0:T(8,128)(2,1)}), bf16[16,72,2048]{2,1,0:T(8,128)(2,1)}, u32[]{:S(2)}, u32[]{:S(2)}) async-start(bf16[16,72,2048]{2,1,0:T(8,128)(2,1)} %broadcast_select_fusion), calls=%async_computation | async-start | bytes 9437184 | tf_op jit(solution)/shard_map/all_to_all | solution.py:39
  52.5 12.5 %gather_fusion.4 = bf16[1152,2048]{1,0:T(8,128)(2,1)} fusion(bf16[512,2048]{1,0:T(8,128)(2,1)} %all-gather.2.cloned.1.call-done, s32[2048]{0:T(1024)S(1)} %pad_clamp_fusion.1), kind=kCustom, calls=%fused_computation.4 | custom fusion | bytes 9441792 | tf_op jit(solution)/shard_map/gather | solution.py:103
  70.4 40.8 %all-to-all-done = bf16[16,72,2048]{2,1,0:T(8,128)(2,1)} async-done(((bf16[16,72,2048]{2,1,0:T(8,128)(2,1)}), bf16[16,72,2048]{2,1,0:T(8,128)(2,1)}, u32[]{:S(2)}, u32[]{:S(2)}) %all-to-all-start) | async-done | bytes 4718624 | tf_op jit(solution)/shard_map/all_to_all | solution.py:39
  111.1 9.9 %all-to-all-start.1 = ((bf16[16,72,2048]{2,1,0:T(8,128)(2,1)}), bf16[16,72,2048]{2,1,0:T(8,128)(2,1)}, u32[]{:S(2)}, u32[]{:S(2)}) async-start(bf16[16,72,2048]{2,1,0:T(8,128)(2,1)} %fusion), calls=%async_computation.2 | async-start | bytes 9437184 | tf_op jit(solution)/shard_map/all_to_all | solution.py:39
  122.9 11.3 %mul.105 = f32[512,6,2048]{2,1,0:T(8,128)} broadcast(bf16[512,2048]{1,0:T(8,128)(2,1)S(1)} %copy-done.2), dimensions={0,2} | broadcast | bytes 27262976 | tf_op jit(solution)/shard_map/mul | solution.py:98
  134.2 29.7 %mul.106 = f32[3072,2048]{1,0:T(8,128)} reshape(f32[512,6,2048]{2,1,0:T(8,128)} %mul.105) | data formatting | bytes 50331648 | tf_op jit(solution)/shard_map/mul | solution.py:98
  175.2 7.7 %all-to-all-done.1 = bf16[16,72,2048]{2,1,0:T(8,128)(2,1)} async-done(((bf16[16,72,2048]{2,1,0:T(8,128)(2,1)}), bf16[16,72,2048]{2,1,0:T(8,128)(2,1)}, u32[]{:S(2)}, u32[]{:S(2)}) %all-to-all-start.1) | async-done | bytes 4718624 | tf_op jit(solution)/shard_map/all_to_all | solution.py:39
  240.7 7.1 collective-permute-done.3
  278.3 9.1 %collective-permute-done.7 = bf16[1,72,2048]{2,1,0:T(8,128)(2,1)S(1)} collective-permute-done((bf16[1,72,2048]{2,1,0:T(8,128)(2,1)S(1)}, bf16[1,72,2048]{2,1,0:T(8,128)(2,1)S(1)}, u32[]{:S(2)}, u32[]{:S(2)}) %collective-permute-start.7) | collective-permute-done | bytes 294944 | tf_op jit(solution)/shard_map/ppermute | solution.py:27
  302.2 7.7 %collective-permute-done.9 = bf16[1,72,2048]{2,1,0:T(8,128)(2,1)S(1)} collective-permute-done((bf16[1,72,2048]{2,1,0:T(8,128)(2,1)S(1)}, bf16[1,72,2048]{2,1,0:T(8,128)(2,1)S(1)}, u32[]{:S(2)}, u32[]{:S(2)}) %collective-permute-start.9) | collective-permute-done | bytes 294944 | tf_op jit(solution)/shard_map/ppermute | solution.py:27
  312.4 14.1 %collective-permute-done.10 = bf16[1,72,2048]{2,1,0:T(8,128)(2,1)S(1)} collective-permute-done((bf16[1,72,2048]{2,1,0:T(8,128)(2,1)S(1)}, bf16[1,72,2048]{2,1,0:T(8,128)(2,1)S(1)}, u32[]{:S(2)}, u32[]{:S(2)}) %collective-permute-start.10) | collective-permute-done | bytes 294944 | tf_op jit(solution)/shard_map/ppermute | solution.py:27
  363.1 9.2 %collective-permute-start.18 = (bf16[1,72,2048]{2,1,0:T(8,128)(2,1)}, bf16[1,72,2048]{2,1,0:T(8,128)(2,1)S(1)}, u32[]{:S(2)}, u32[]{:S(2)}) collective-permute-start(bf16[1,72,2048]{2,1,0:T(8,128)(2,1)} %get-tuple-element.28), channel_id=1, source_target_pairs={{0,64},{16,80},{32,96},{48,112},{64,0},{80,16},{96,32},{112,48},{1... | collective-permute-start | bytes 884744 | tf_op jit(solution)/shard_map/ppermute | solution.py:27
  391.1 8.2 %collective-permute-done.20 = bf16[1,72,2048]{2,1,0:T(8,128)(2,1)S(1)} collective-permute-done((bf16[1,72,2048]{2,1,0:T(8,128)(2,1)}, bf16[1,72,2048]{2,1,0:T(8,128)(2,1)S(1)}, u32[]{:S(2)}, u32[]{:S(2)}) %collective-permute-start.20) | collective-permute-done | bytes 294944 | tf_op jit(solution)/shard_map/ppermute | solution.py:27
  431.0 7.2 collective-permute-done.24
  460.3 26.8 %gather_fusion.2 = bf16[3072,2048]{1,0:T(8,128)(2,1)} fusion(bf16[1152,2048]{1,0:T(8,128)(2,1)} %bitcast.182, s32[3072]{0:T(1024)S(1)} %broadcast_clamp_fusion), kind=kCustom, calls=%fused_computation.2 | custom fusion | bytes 25178112 | tf_op jit(solution)/shard_map/gather | solution.py:92
  487.1 26.7 %gather_fusion.6 = bf16[3072,2048]{1,0:T(8,128)(2,1)} fusion(bf16[1152,2048]{1,0:T(8,128)(2,1)} %bitcast.183, s32[3072]{0:T(1024)S(1)} %broadcast_clamp_fusion), kind=kCustom, calls=%fused_computation.6 | custom fusion | bytes 25178112 | tf_op jit(solution)/shard_map/gather | solution.py:121
  513.9 20.3 %gather.39 = bf16[512,6,2048]{2,1,0:T(8,128)(2,1)} reshape(bf16[3072,2048]{1,0:T(8,128)(2,1)} %gather_fusion.6) | data formatting | bytes 25165824 | tf_op jit(solution)/shard_map/gather | solution.py:121
  534.2 13.1 %multiply_reduce_fusion.1 = bf16[3072]{0:T(1024)(128)(2,1)S(1)} fusion(f32[3072,2048]{1,0:T(8,128)} %mul.106, bf16[3072,2048]{1,0:T(8,128)(2,1)} %gather_fusion.2, pred[3072]{0:T(1024)(128)(4,1)S(1)} %broadcast_compare_fusion), kind=kLoop, calls=%fused_computation.9 | loop fusion | flops 25162752 | bytes 37757952 | tf_op jit(solution)/shard_map/reduce_sum | solution.py:97
  548.5 14.2 %select_reduce_fusion = bf16[512,2048]{1,0:T(8,128)(2,1)} fusion(bf16[512,6,2048]{2,1,0:T(8,128)(2,1)} %gather.39, pred[512,6]{1,0:T(8,128)(4,1)S(1)} %copy-done.10), kind=kLoop, calls=%fused_computation.10 | loop fusion | flops 11534336 | bytes 14683136 | tf_op jit(solution)/shard_map/reduce_sum | solution.py:122
  562.8 20.4 %gather.33 = bf16[512,6,2048]{2,1,0:T(8,128)(2,1)} reshape(bf16[3072,2048]{1,0:T(8,128)(2,1)} %gather_fusion.2) | data formatting | bytes 25165824 | tf_op jit(solution)/shard_map/gather | solution.py:92
  583.2 20.6 %multiply_reduce_fusion = bf16[512,2048]{1,0:T(8,128)(2,1)} fusion(bf16[512,6,2048]{2,1,0:T(8,128)(2,1)} %gather.33, f32[512,6]{1,0:T(8,128)S(1)} %copy-done.4, pred[512,6]{1,0:T(8,128)(4,1)S(1)} %copy-done.10), kind=kLoop, calls=%fused_computation.8 | loop fusion | flops 24117248 | bytes 14695424 | tf_op jit(solution)/shard_map/reduce_sum | solution.py:95
  621.9 48.3 %reduce-scatter.6.cloned.1.call-done = bf16[32,2048]{1,0:T(8,128)(2,1)} async-done(((bf16[512,2048]{1,0:T(8,128)(2,1)}), bf16[32,2048]{1,0:T(8,128)(2,1)}) %reduce-scatter.6.cloned.1.call-update) | async-done | bytes 131088 | tf_op jit(solution)/shard_map/reduce_scatter | solution.py:129
  670.3 61.0 %reduce-scatter.4.cloned.1.call-done = bf16[32,2048]{1,0:T(8,128)(2,1)} async-done(((bf16[512,2048]{1,0:T(8,128)(2,1)}), bf16[32,2048]{1,0:T(8,128)(2,1)}) %reduce-scatter.4.cloned.1.call-update) | async-done | bytes 131088 | tf_op jit(solution)/shard_map/reduce_scatter | solution.py:126
  (169 shorter events, 278.1 us)
Async XLA Ops:
  7.2 45.3 %all-gather.2.cloned.1.call-start = ((), (), s32[]{:S(2)}) async-start(), calls=%async_computation.6 | async-start | bytes 2228224 | tf_op jit(solution)/shard_map/all_gather | solution.py:96
  37.7 73.5 %all-to-all-start = ((bf16[16,72,2048]{2,1,0:T(8,128)(2,1)}), bf16[16,72,2048]{2,1,0:T(8,128)(2,1)}, u32[]{:S(2)}, u32[]{:S(2)}) async-start(bf16[16,72,2048]{2,1,0:T(8,128)(2,1)} %broadcast_select_fusion), calls=%async_computation | async-start | bytes 9437184 | tf_op jit(solution)/shard_map/all_to_all | solution.py:39
  111.1 71.8 %all-to-all-start.1 = ((bf16[16,72,2048]{2,1,0:T(8,128)(2,1)}), bf16[16,72,2048]{2,1,0:T(8,128)(2,1)}, u32[]{:S(2)}, u32[]{:S(2)}) async-start(bf16[16,72,2048]{2,1,0:T(8,128)(2,1)} %fusion), calls=%async_computation.2 | async-start | bytes 9437184 | tf_op jit(solution)/shard_map/all_to_all | solution.py:39
  121.1 499.5 %reduce-scatter.8.cloned.1.call-start = ((), (), s32[]{:S(2)}) async-start(), calls=%async_computation.8 | async-start | bytes 139264 | tf_op jit(solution)/shard_map/reduce_scatter | solution.py:132
  193.3 145.0 %collective-permute-start.14 = (bf16[1,72,2048]{2,1,0:T(8,128)(2,1)S(1)}, bf16[1,72,2048]{2,1,0:T(8,128)(2,1)S(1)}, u32[]{:S(2)}, u32[]{:S(2)}) collective-permute-start(bf16[1,72,2048]{2,1,0:T(8,128)(2,1)S(1)} %get-tuple-element.33), channel_id=1, source_target_pairs={{0,240},{16,224},{32,208},{48,192},{64,176},{80,160},{96,144},{112... | collective-permute-start | bytes 884744 | tf_op jit(solution)/shard_map/ppermute | solution.py:27
  197.6 136.5 %collective-permute-start.13 = (bf16[1,72,2048]{2,1,0:T(8,128)(2,1)S(1)}, bf16[1,72,2048]{2,1,0:T(8,128)(2,1)S(1)}, u32[]{:S(2)}, u32[]{:S(2)}) collective-permute-start(bf16[1,72,2048]{2,1,0:T(8,128)(2,1)S(1)} %get-tuple-element.34), channel_id=1, source_target_pairs={{0,224},{16,240},{32,192},{48,208},{64,160},{80,176},{96,128},{112... | collective-permute-start | bytes 884744 | tf_op jit(solution)/shard_map/ppermute | solution.py:27
  201.8 130.1 %collective-permute-start.12 = (bf16[1,72,2048]{2,1,0:T(8,128)(2,1)S(1)}, bf16[1,72,2048]{2,1,0:T(8,128)(2,1)S(1)}, u32[]{:S(2)}, u32[]{:S(2)}) collective-permute-start(bf16[1,72,2048]{2,1,0:T(8,128)(2,1)S(1)} %get-tuple-element.35), channel_id=1, source_target_pairs={{0,208},{16,192},{32,240},{48,224},{64,144},{80,128},{96,176},{112... | collective-permute-start | bytes 884744 | tf_op jit(solution)/shard_map/ppermute | solution.py:27
  201.8 125.4 %collective-permute-start.11 = (bf16[1,72,2048]{2,1,0:T(8,128)(2,1)S(1)}, bf16[1,72,2048]{2,1,0:T(8,128)(2,1)S(1)}, u32[]{:S(2)}, u32[]{:S(2)}) collective-permute-start(bf16[1,72,2048]{2,1,0:T(8,128)(2,1)S(1)} %get-tuple-element.36), channel_id=1, source_target_pairs={{0,192},{16,208},{32,224},{48,240},{64,128},{80,144},{96,160},{112... | collective-permute-start | bytes 884744 | tf_op jit(solution)/shard_map/ppermute | solution.py:27
  202.9 16.8 %collective-permute-start = (bf16[1,72,2048]{2,1,0:T(8,128)(2,1)S(1)}, bf16[1,72,2048]{2,1,0:T(8,128)(2,1)S(1)}, u32[]{:S(2)}, u32[]{:S(2)}) collective-permute-start(bf16[1,72,2048]{2,1,0:T(8,128)(2,1)S(1)} %get-tuple-element.47), channel_id=1, source_target_pairs={{0,16},{16,0},{32,48},{48,32},{64,80},{80,64},{96,112},{112,96},{1... | collective-permute-start | bytes 884744 | tf_op jit(solution)/shard_map/ppermute | solution.py:27
  247.9 11.4 %collective-permute-start.4 = (bf16[1,72,2048]{2,1,0:T(8,128)(2,1)S(1)}, bf16[1,72,2048]{2,1,0:T(8,128)(2,1)S(1)}, u32[]{:S(2)}, u32[]{:S(2)}) collective-permute-start(bf16[1,72,2048]{2,1,0:T(8,128)(2,1)S(1)} %get-tuple-element.43), channel_id=1, source_target_pairs={{0,80},{16,64},{32,112},{48,96},{64,16},{80,0},{96,48},{112,32},{1... | collective-permute-start | bytes 884744 | tf_op jit(solution)/shard_map/ppermute | solution.py:27
  276.0 11.4 %collective-permute-start.7 = (bf16[1,72,2048]{2,1,0:T(8,128)(2,1)S(1)}, bf16[1,72,2048]{2,1,0:T(8,128)(2,1)S(1)}, u32[]{:S(2)}, u32[]{:S(2)}) collective-permute-start(bf16[1,72,2048]{2,1,0:T(8,128)(2,1)S(1)} %get-tuple-element.40), channel_id=1, source_target_pairs={{0,128},{16,144},{32,160},{48,176},{64,192},{80,208},{96,224},{112... | collective-permute-start | bytes 884744 | tf_op jit(solution)/shard_map/ppermute | solution.py:27
  287.4 11.8 %collective-permute-start.8 = (bf16[1,72,2048]{2,1,0:T(8,128)(2,1)S(1)}, bf16[1,72,2048]{2,1,0:T(8,128)(2,1)S(1)}, u32[]{:S(2)}, u32[]{:S(2)}) collective-permute-start(bf16[1,72,2048]{2,1,0:T(8,128)(2,1)S(1)} %get-tuple-element.39), channel_id=1, source_target_pairs={{0,144},{16,128},{32,176},{48,160},{64,208},{80,192},{96,240},{112... | collective-permute-start | bytes 884744 | tf_op jit(solution)/shard_map/ppermute | solution.py:27
  299.1 10.7 %collective-permute-start.9 = (bf16[1,72,2048]{2,1,0:T(8,128)(2,1)S(1)}, bf16[1,72,2048]{2,1,0:T(8,128)(2,1)S(1)}, u32[]{:S(2)}, u32[]{:S(2)}) collective-permute-start(bf16[1,72,2048]{2,1,0:T(8,128)(2,1)S(1)} %get-tuple-element.38), channel_id=1, source_target_pairs={{0,160},{16,176},{32,128},{48,144},{64,224},{80,240},{96,192},{112... | collective-permute-start | bytes 884744 | tf_op jit(solution)/shard_map/ppermute | solution.py:27
  309.9 16.7 %collective-permute-start.10 = (bf16[1,72,2048]{2,1,0:T(8,128)(2,1)S(1)}, bf16[1,72,2048]{2,1,0:T(8,128)(2,1)S(1)}, u32[]{:S(2)}, u32[]{:S(2)}) collective-permute-start(bf16[1,72,2048]{2,1,0:T(8,128)(2,1)S(1)} %get-tuple-element.37), channel_id=1, source_target_pairs={{0,176},{16,160},{32,144},{48,128},{64,240},{80,224},{96,208},{112... | collective-permute-start | bytes 884744 | tf_op jit(solution)/shard_map/ppermute | solution.py:27
  326.5 126.6 %collective-permute-start.29 = (bf16[1,72,2048]{2,1,0:T(8,128)(2,1)S(1)}, bf16[1,72,2048]{2,1,0:T(8,128)(2,1)}, u32[]{:S(2)}, u32[]{:S(2)}) collective-permute-start(bf16[1,72,2048]{2,1,0:T(8,128)(2,1)S(1)} %get-tuple-element.17), channel_id=1, source_target_pairs={{0,240},{16,224},{32,208},{48,192},{64,176},{80,160},{96,144},{112... | collective-permute-start | bytes 884744 | tf_op jit(solution)/shard_map/ppermute | solution.py:27
  327.3 124.2 %collective-permute-start.28 = (bf16[1,72,2048]{2,1,0:T(8,128)(2,1)S(1)}, bf16[1,72,2048]{2,1,0:T(8,128)(2,1)}, u32[]{:S(2)}, u32[]{:S(2)}) collective-permute-start(bf16[1,72,2048]{2,1,0:T(8,128)(2,1)S(1)} %get-tuple-element.18), channel_id=1, source_target_pairs={{0,224},{16,240},{32,192},{48,208},{64,160},{80,176},{96,128},{112... | collective-permute-start | bytes 884744 | tf_op jit(solution)/shard_map/ppermute | solution.py:27
  331.9 117.8 %collective-permute-start.27 = (bf16[1,72,2048]{2,1,0:T(8,128)(2,1)S(1)}, bf16[1,72,2048]{2,1,0:T(8,128)(2,1)}, u32[]{:S(2)}, u32[]{:S(2)}) collective-permute-start(bf16[1,72,2048]{2,1,0:T(8,128)(2,1)S(1)} %get-tuple-element.19), channel_id=1, source_target_pairs={{0,208},{16,192},{32,240},{48,224},{64,144},{80,128},{96,176},{112... | collective-permute-start | bytes 884744 | tf_op jit(solution)/shard_map/ppermute | solution.py:27
  334.0 114.0 %collective-permute-start.26 = (bf16[1,72,2048]{2,1,0:T(8,128)(2,1)S(1)}, bf16[1,72,2048]{2,1,0:T(8,128)(2,1)}, u32[]{:S(2)}, u32[]{:S(2)}) collective-permute-start(bf16[1,72,2048]{2,1,0:T(8,128)(2,1)S(1)} %get-tuple-element.20), channel_id=1, source_target_pairs={{0,192},{16,208},{32,224},{48,240},{64,128},{80,144},{96,160},{112... | collective-permute-start | bytes 884744 | tf_op jit(solution)/shard_map/ppermute | solution.py:27
  363.1 16.2 %collective-permute-start.18 = (bf16[1,72,2048]{2,1,0:T(8,128)(2,1)}, bf16[1,72,2048]{2,1,0:T(8,128)(2,1)S(1)}, u32[]{:S(2)}, u32[]{:S(2)}) collective-permute-start(bf16[1,72,2048]{2,1,0:T(8,128)(2,1)} %get-tuple-element.28), channel_id=1, source_target_pairs={{0,64},{16,80},{32,96},{48,112},{64,0},{80,16},{96,32},{112,48},{1... | collective-permute-start | bytes 884744 | tf_op jit(solution)/shard_map/ppermute | solution.py:27
  387.1 12.3 %collective-permute-start.20 = (bf16[1,72,2048]{2,1,0:T(8,128)(2,1)}, bf16[1,72,2048]{2,1,0:T(8,128)(2,1)S(1)}, u32[]{:S(2)}, u32[]{:S(2)}) collective-permute-start(bf16[1,72,2048]{2,1,0:T(8,128)(2,1)} %get-tuple-element.26), channel_id=1, source_target_pairs={{0,96},{16,112},{32,64},{48,80},{64,32},{80,48},{96,0},{112,16},{1... | collective-permute-start | bytes 884744 | tf_op jit(solution)/shard_map/ppermute | solution.py:27
  416.7 10.9 %collective-permute-start.23 = (bf16[1,72,2048]{2,1,0:T(8,128)(2,1)S(1)}, bf16[1,72,2048]{2,1,0:T(8,128)(2,1)S(1)}, u32[]{:S(2)}, u32[]{:S(2)}) collective-permute-start(bf16[1,72,2048]{2,1,0:T(8,128)(2,1)S(1)} %get-tuple-element.23), channel_id=1, source_target_pairs={{0,144},{16,128},{32,176},{48,160},{64,208},{80,192},{96,240},{112... | collective-permute-start | bytes 884744 | tf_op jit(solution)/shard_map/ppermute | solution.py:27
  427.6 10.6 %collective-permute-start.24 = (bf16[1,72,2048]{2,1,0:T(8,128)(2,1)S(1)}, bf16[1,72,2048]{2,1,0:T(8,128)(2,1)S(1)}, u32[]{:S(2)}, u32[]{:S(2)}) collective-permute-start(bf16[1,72,2048]{2,1,0:T(8,128)(2,1)S(1)} %get-tuple-element.22), channel_id=1, source_target_pairs={{0,160},{16,176},{32,128},{48,144},{64,224},{80,240},{96,192},{112... | collective-permute-start | bytes 884744 | tf_op jit(solution)/shard_map/ppermute | solution.py:27
  548.3 122.0 %reduce-scatter.6.cloned.1.call-start = ((), (), s32[]{:S(2)}) async-start(), calls=%async_computation.7 | async-start | bytes 2228224 | tf_op jit(solution)/shard_map/reduce_scatter | solution.py:129
  562.8 168.5 %reduce-scatter.4.cloned.1.call-start = ((), (), s32[]{:S(2)}) async-start(), calls=%async_computation.5 | async-start | bytes 2228224 | tf_op jit(solution)/shard_map/reduce_scatter | solution.py:126
  (27 other events, 452.3 us)
Sparse Core Ops, SparseCore 0:
  9.8 42.5 all-gather.1
  548.4 60.7 reduce-scatter.7
  612.4 57.7 reduce-scatter.5
  673.4 57.8 reduce-scatter.3
